TPU v7x, 32 devices: a whole 2x2x4 slice. The times are simulated.
32 devices in a mesh: outer: 4 (over y, x), inner: 8 (over z, core).
Axes of the slice: x: 2, y: 2, z: 4, core: 2. Of those that a mesh axis runs over, the one named last changes fastest.
Arguments:
- points: float32 [3584, 256], P(('outer', 'inner')), may hold values from -36 to 36
- vectors: float32 [3584, 128], P(('outer', 'inner')), may hold values from -6 to 6
- lengthscales: float32 [256], replicated, may hold values from 8 to 32
- outputscale: float32 [1], replicated, may hold values from 0.03 to 0.12
- noise: float32 [1], replicated, may hold values from 0.3 to 3
Outputs:
- product: float32 [3584, 128], P(('outer', 'inner'))
All inputs are finite; a program needn't handle non-finite values.
Results may differ from a plain program's by a relative error of at most 0.00024.
Values sent between devices are 32-bit elements; how exact they have to be, the bound alone decides.
No kernel may reach another device: no remote copies, remote signals or barrier semaphores. Data moves between devices by JAX's collectives and lax.ppermute only.
A program may use at most 128 MiB of HBM per device.

v0:
```python
import jax
import jax.numpy as jnp
from jax import lax
from jax.sharding import PartitionSpec as P


def matern(dist2, amplitude):
    scaled_r = jnp.sqrt(5.0) * jnp.sqrt(jnp.maximum(dist2, 0.0))
    return amplitude * (1.0 + scaled_r + scaled_r * scaled_r / 3.0) * jnp.exp(-scaled_r)


def row_norms(rows):
    return jnp.sum(rows * rows, axis=1)


def kernel_tile(rows, norms_here, cols, col_norms, amplitude):
    inner_prod = jnp.dot(
        rows, cols.T, precision=lax.Precision.HIGHEST, preferred_element_type=jnp.float32
    )
    dist2 = norms_here[:, None] + col_norms[None, :] - 2.0 * inner_prod
    return matern(dist2, amplitude)


def apply_tile(tile, values):
    return jnp.dot(
        tile, values, precision=lax.Precision.HIGHEST, preferred_element_type=jnp.float32
    )


def per_device(points, vectors, lengthscales, outputscale, noise):
    amplitude = outputscale[0]
    scaled = points / lengthscales[None, :]
    sqnorm = row_norms(scaled)
    piece_rows = lax.all_gather(scaled, ("outer", "inner"), axis=0, tiled=True)
    piece_values = lax.all_gather(vectors, ("outer", "inner"), axis=0, tiled=True)
    tile = kernel_tile(scaled, sqnorm, piece_rows, row_norms(piece_rows), amplitude)
    total = apply_tile(tile, piece_values)
    return total + noise[0] * vectors


def solution(mesh):
    placed = (P(("outer", "inner"), None), P(("outer", "inner"), None), P(), P(), P())
    return jax.shard_map(
        per_device,
        mesh=mesh,
        in_specs=placed,
        out_specs=P(("outer", "inner"), None),
        check_vma=False,
    )
```

profile of v0, /device:TPU:0, one launch (start us, length us, event | category | flops | bytes accessed | tf_op | source)
XLA Modules:
  0.0 142.2 jit_solution(13806589943837288145)
XLA Ops:
  6.5 0.0 all-gather.3.cloned.1.call-start
  6.5 1.7 %multiply_reduce_fusion.1 = (f32[112]{0:T(128)S(1)}, f32[112,256]{1,0:T(8,128)}) fusion(f32[112,256]{1,0:T(8,128)} %param.5, f32[256]{0:T(256)} %param.7), kind=kLoop, calls=%fused_computation.19 | loop fusion | flops 85904 | bytes 230848 | tf_op jit(solution)/shard_map/reduce_sum | solution.py:13
  8.2 0.0 copy-start.1
  8.2 0.0 all-gather.3.cloned.1.call-update
  8.2 0.0 all-gather.5.cloned.1.call-start
  8.3 0.7 all-gather.5.cloned.1.call-update
  10.3 63.2 %all-gather.3.cloned.1.call-done = f32[3584,256]{1,0:T(8,128)} async-done(((f32[112,256]{1,0:T(8,128)}), f32[3584,256]{1,0:T(8,128)}) %all-gather.3.cloned.1.call-update) | async-done | bytes 3670032 | tf_op jit(solution)/shard_map/all_gather | solution.py:34
  73.5 0.0 copy-start
  73.5 2.7 %multiply_reduce_fusion = f32[3584]{0:T(1024)S(1)} fusion(f32[3584,256]{1,0:T(8,128)} %all-gather.3.cloned.1.call-done), kind=kLoop, calls=%fused_computation.5 | loop fusion | flops 1831424 | bytes 3684352 | tf_op jit(solution)/shard_map/reduce_sum | solution.py:13
  76.2 0.0 copy-done.1
  76.3 0.4 copy-done
  76.6 0.0 copy-start.2
  76.7 4.0 %fusion.3 = f32[112,3584]{1,0:T(8,128)S(1)} fusion(f32[112,256]{1,0:T(8,128)S(1)} %copy-done.1, f32[3584,256]{1,0:T(8,128)S(1)} %copy-done, f32[3584]{0:T(1024)S(1)} %multiply_reduce_fusion, f32[112]{0:T(128)S(1)} %get-tuple-element.5), kind=kOutput, calls=%fused_computation.4 | convolution fusion | flops 1235132416 | bytes 5405120 | tf_op jit(solution)/shard_map/dot_general | solution.py:17
  80.6 50.5 %all-gather.5.cloned.1.call-done = f32[3584,128]{1,0:T(8,128)} async-done(((f32[112,128]{1,0:T(8,128)}), f32[3584,128]{1,0:T(8,128)}) %all-gather.5.cloned.1.call-update) | async-done | bytes 1835024 | tf_op jit(solution)/shard_map/all_gather | solution.py:35
  131.2 0.0 copy-done.2
  131.2 4.2 %fusion.13 = f32[112,128]{1,0:T(8,128)} fusion(f32[3584,128]{1,0:T(8,128)} %all-gather.5.cloned.1.call-done, f32[112,3584]{1,0:T(8,128)S(1)} %fusion.3, f32[]{:T(128)} %bitcast.5, f32[112,128]{1,0:T(8,128)S(1)} %copy-done.2, f32[]{:T(128)} %bitcast.6), kind=kOutput, calls=%fused_computation.15 | convolution fusion | flops 619401216 | bytes 3555336 | tf_op jit(solution)/shard_map/dot_general | solution.py:25
Async XLA Ops:
  6.5 67.0 %all-gather.3.cloned.1.call-start = ((), (), s32[]{:S(2)}) async-start(), calls=%async_computation | async-start | bytes 3784704 | tf_op jit(solution)/shard_map/all_gather | solution.py:34
  8.2 68.0 %copy-start.1 = (f32[112,256]{1,0:T(8,128)S(1)}, f32[112,256]{1,0:T(8,128)}, u32[]{:S(2)}) copy-start(f32[112,256]{1,0:T(8,128)} %get-tuple-element.6) | copy-start | bytes 344068
  8.2 122.9 %all-gather.5.cloned.1.call-start = ((), (), s32[]{:S(2)}) async-start(), calls=%async_computation.1 | async-start | bytes 1892352 | tf_op jit(solution)/shard_map/all_gather | solution.py:35
  73.5 3.1 %copy-start = (f32[3584,256]{1,0:T(8,128)S(1)}, f32[3584,256]{1,0:T(8,128)}, u32[]{:S(2)}) copy-start(f32[3584,256]{1,0:T(8,128)} %all-gather.3.cloned.1.call-done) | copy-start | bytes 11010052
  76.6 54.5 %copy-start.2 = (f32[112,128]{1,0:T(8,128)S(1)}, f32[112,128]{1,0:T(8,128)}, u32[]{:S(2)}) copy-start(f32[112,128]{1,0:T(8,128)} %param.6) | copy-start | bytes 172036
Sparse Core Ops, SparseCore 0:
  10.2 63.2 all-gather.2
  76.4 54.7 all-gather.4
where the time goes:
time: 142 us
  waiting for transfers between devices  114 us (80%)
  between operations  14.7 us (10%)
  matrix products  8.21 us (6%)
  other arithmetic  4.39 us (3%)
    all_gather x1, waiting for transfers between devices, per_device(): piece_rows = lax.all_gather(scaled, ('outer', 'inner'), axis=0, tiled=True)  63.2 us
    all_gather x1, waiting for transfers between devices, per_device(): lax.all_gather(vectors, ('outer', 'inner'), axis=0, tiled=True)  50.5 us
    reduce_sum x2, other arithmetic, row_norms(): return jnp.sum(rows * rows, axis=1)  4.39 us
    dot_general x1, matrix products, apply_tile(): jnp.dot(tile, values, precision=lax.Precision.HIGHEST, preferred_element_...  4.23 us
    dot_general x1, matrix products, kernel_tile(): jnp.dot(rows, cols.T, precision=lax.Precision.HIGHEST, preferred_element_...  3.97 us
  transfers between devices with their start and end apart: 2, of which 2 were waited for; matrix products, arithmetic and copies ran while one was open for 5% of the time, Pallas kernels for 0%

commit v1 on v0

--- a/solution.py
+++ b/solution.py
@@ -31,8 +31,13 @@
     amplitude = outputscale[0]
     scaled = points / lengthscales[None, :]
     sqnorm = row_norms(scaled)
-    piece_rows = lax.all_gather(scaled, ("outer", "inner"), axis=0, tiled=True)
-    piece_values = lax.all_gather(vectors, ("outer", "inner"), axis=0, tiled=True)
+    piece_rows, piece_values = jnp.split(
+        lax.all_gather(
+            jnp.concatenate([scaled, vectors], axis=1), ("outer", "inner"), axis=0, tiled=True
+        ),
+        [scaled.shape[1]],
+        axis=1,
+    )
     tile = kernel_tile(scaled, sqnorm, piece_rows, row_norms(piece_rows), amplitude)
     total = apply_tile(tile, piece_values)
     return total + noise[0] * vectors

time: 142 us -> 99.4 us (0.70)
  waiting for transfers between devices: 114 us -> 69 us
  matrix products: 8.21 us -> 10.2 us
    all_gather x2 -> x1, waiting for transfers between devices: 114 us -> 69 us  [per_device(): lax.all_gather(jnp.concatenate([scaled, vectors], axis=1), ('outer', 'inn...]
    dot_general x1, matrix products: 3.97 us -> 5.97 us  [kernel_tile(): jnp.dot(rows, cols.T, precision=lax.Precision.HIGHEST, preferred_element_...]
    concatenate x0 -> x1, other arithmetic: none -> 1.53 us  [per_device(): jnp.concatenate([scaled, vectors], axis=1)]
  transfers between devices with their start and end apart: 2 -> 1, of which waited for: 2 -> 1; matrix products, arithmetic and copies ran while one was open for 5% -> 0% of each run, Pallas kernels for 0% -> 0%
where the time goes in v1:
time: 99.4 us; the launch traced here: 99.1 us
  waiting for transfers between devices  69 us (69%)
  between operations  14.7 us (15%)
  matrix products  10.2 us (10%)
  other arithmetic  5.13 us (5%)
    all_gather x1, waiting for transfers between devices, per_device(): lax.all_gather(jnp.concatenate([scaled, vectors], axis=1), ('outer', 'inn...  69 us
    dot_general x1, matrix products, kernel_tile(): jnp.dot(rows, cols.T, precision=lax.Precision.HIGHEST, preferred_element_...  5.97 us
    dot_general x1, matrix products, apply_tile(): jnp.dot(tile, values, precision=lax.Precision.HIGHEST, preferred_element_...  4.25 us
    reduce_sum x2, other arithmetic, row_norms(): return jnp.sum(rows * rows, axis=1)  3.6 us
  transfers between devices with their start and end apart: 1, of which 1 were waited for; matrix products, arithmetic and copies ran while one was open for 0% of the time, Pallas kernels for 0%

profile of v1, /device:TPU:0, one launch (start us, length us, event | category | flops | bytes accessed | tf_op | source)
XLA Modules:
  0.0 99.1 jit_solution(16321836968841525906)
XLA Ops:
  6.5 0.0 all-gather.2.cloned.1.call-start
  6.5 1.0 %multiply_reduce_fusion.1 = (f32[112]{0:T(128)S(1)}, f32[112,256]{1,0:T(8,128)S(1)}) fusion(f32[112,256]{1,0:T(8,128)} %param.5, f32[256]{0:T(256)} %param.7), kind=kLoop, calls=%fused_computation.22 | loop fusion | flops 85904 | bytes 230848 | tf_op jit(solution)/shard_map/reduce_sum | solution.py:13
  7.6 1.5 %pad_maximum_fusion = f32[112,384]{1,0:T(8,128)} fusion(f32[112,128]{1,0:T(8,128)} %param.6, f32[112,256]{1,0:T(8,128)S(1)} %get-tuple-element.6), kind=kLoop, calls=%fused_computation.21 | loop fusion | flops 43008 | bytes 344064 | tf_op jit(solution)/shard_map/concatenate | solution.py:36
  9.1 0.0 all-gather.2.cloned.1.call-update
  10.4 69.0 %all-gather.2.cloned.1.call-done = f32[3584,384]{1,0:T(8,128)} async-done(((f32[112,384]{1,0:T(8,128)}), f32[3584,384]{1,0:T(8,128)}) %all-gather.2.cloned.1.call-update) | async-done | bytes 5505040 | tf_op jit(solution)/shard_map/all_gather | solution.py:35
  79.4 2.6 %multiply_reduce_fusion = f32[3584]{0:T(1024)S(1)} fusion(f32[3584,384]{1,0:T(8,128)} %all-gather.2.cloned.1.call-done), kind=kLoop, calls=%fused_computation.5 | loop fusion | flops 1831424 | bytes 3684352 | tf_op jit(solution)/shard_map/reduce_sum | solution.py:13
  82.0 0.0 copy-start
  82.0 6.0 %fusion.3 = f32[112,3584]{1,0:T(8,128)S(1)} fusion(f32[112,256]{1,0:T(8,128)S(1)} %get-tuple-element.6, f32[3584,384]{1,0:T(8,128)} %all-gather.2.cloned.1.call-done, f32[3584]{0:T(1024)S(1)} %multiply_reduce_fusion, f32[112]{0:T(128)S(1)} %get-tuple-element.5), kind=kOutput, calls=%fused_computation.4 | convolution fusion | flops 1235132416 | bytes 5405120 | tf_op jit(solution)/shard_map/dot_general | solution.py:17
  88.0 0.0 copy-done
  88.0 4.3 %fusion.15 = f32[112,128]{1,0:T(8,128)} fusion(f32[3584,384]{1,0:T(8,128)} %all-gather.2.cloned.1.call-done, f32[112,3584]{1,0:T(8,128)S(1)} %fusion.3, f32[]{:T(128)} %bitcast.3, f32[112,128]{1,0:T(8,128)S(1)} %copy-done, f32[]{:T(128)} %bitcast.4), kind=kOutput, calls=%fused_computation.17 | convolution fusion | flops 619401216 | bytes 3556352 | tf_op jit(solution)/shard_map/dot_general | solution.py:25
Async XLA Ops:
  6.5 72.9 %all-gather.2.cloned.1.call-start = ((), (), s32[]{:S(2)}) async-start(), calls=%async_computation | async-start | bytes 5677056 | tf_op jit(solution)/shard_map/all_gather | solution.py:35
  82.0 6.0 %copy-start = (f32[112,128]{1,0:T(8,128)S(1)}, f32[112,128]{1,0:T(8,128)}, u32[]{:S(2)}) copy-start(f32[112,128]{1,0:T(8,128)} %param.6) | copy-start | bytes 172036
Sparse Core Ops, SparseCore 0:
  10.4 68.9 all-gather.1

commit v2 on v0

--- a/solution.py
+++ b/solution.py
@@ -2,6 +2,28 @@
 import jax.numpy as jnp
 from jax import lax
 from jax.sharding import PartitionSpec as P
+
+
+def in_order(blocks, dim):
+    lengths = list(blocks.shape[1:])
+    lengths[dim] *= blocks.shape[0]
+    return jnp.moveaxis(blocks, 0, dim).reshape(lengths)
+
+
+def grow_blocks(value, axis):
+    size = lax.axis_size(axis)
+    parts = value[None]
+    for level in range(size.bit_length() - 1):
+        bit = 1 << level
+        other = lax.ppermute(parts, axis, [(i, i ^ bit) for i in range(size)])
+        both = jnp.stack([parts, other])
+        upper = lax.axis_index(axis) >> level & 1
+        parts = jnp.where(upper == 0, both, both[::-1]).reshape(-1, *value.shape)
+    return parts
+
+
+def collect(x, axis, dim):
+    return in_order(grow_blocks(x, axis), dim)
 
 
 def matern(dist2, amplitude):
@@ -32,7 +54,7 @@
     scaled = points / lengthscales[None, :]
     sqnorm = row_norms(scaled)
     piece_rows = lax.all_gather(scaled, ("outer", "inner"), axis=0, tiled=True)
-    piece_values = lax.all_gather(vectors, ("outer", "inner"), axis=0, tiled=True)
+    piece_values = collect(vectors, ("outer", "inner"), 0)
     tile = kernel_tile(scaled, sqnorm, piece_rows, row_norms(piece_rows), amplitude)
     total = apply_tile(tile, piece_values)
     return total + noise[0] * vectors

time: 142 us -> 98.6 us (0.69)
  waiting for transfers between devices: 114 us -> 61.2 us
  starting transfers between devices: 0.04 us -> 8.99 us
  matrix products: 8.21 us -> 6.75 us
    all_gather x1 -> x0, waiting for transfers between devices: 50.5 us -> none  [per_device(): lax.all_gather(vectors, ('outer', 'inner'), axis=0, tiled=True)]
    all_gather x1, waiting for transfers between devices: 63.2 us -> 14.6 us  [per_device(): piece_rows = lax.all_gather(scaled, ('outer', 'inner'), axis=0, tiled=True)]
    ppermute x0 -> x5, waiting for transfers between devices: none -> 46.6 us  [grow_blocks(): other = lax.ppermute(parts, axis, [(i, i ^ bit) for i in range(size)])]
    ppermute x0 -> x5, starting transfers between devices: none -> 8.99 us  [grow_blocks(): other = lax.ppermute(parts, axis, [(i, i ^ bit) for i in range(size)])]
    dot_general x1, matrix products: 4.23 us -> 2.75 us  [apply_tile(): jnp.dot(tile, values, precision=lax.Precision.HIGHEST, preferred_element_...]
  transfers between devices with their start and end apart: 2 -> 6, of which waited for: 2 -> 6; matrix products, arithmetic and copies ran while one was open for 5% -> 1% of each run, Pallas kernels for 0% -> 0%
where the time goes in v2:
time: 98.6 us; the launch traced here: 97.9 us
  waiting for transfers between devices  61.2 us (62%)
  between operations  14.8 us (15%)
  starting transfers between devices  8.99 us (9%)
  matrix products  6.75 us (7%)
  other arithmetic  5.7 us (6%)
    ppermute x5, waiting for transfers between devices, grow_blocks(): other = lax.ppermute(parts, axis, [(i, i ^ bit) for i in range(size)])  46.6 us
    all_gather x1, waiting for transfers between devices, per_device(): piece_rows = lax.all_gather(scaled, ('outer', 'inner'), axis=0, tiled=True)  14.6 us
    ppermute x5, starting transfers between devices, grow_blocks(): other = lax.ppermute(parts, axis, [(i, i ^ bit) for i in range(size)])  8.99 us
    reduce_sum x2, other arithmetic, row_norms(): return jnp.sum(rows * rows, axis=1)  4.39 us
    dot_general x1, matrix products, kernel_tile(): jnp.dot(rows, cols.T, precision=lax.Precision.HIGHEST, preferred_element_...  4 us
    dot_general x1, matrix products, apply_tile(): jnp.dot(tile, values, precision=lax.Precision.HIGHEST, preferred_element_...  2.75 us
  transfers between devices with their start and end apart: 6, of which 6 were waited for; matrix products, arithmetic and copies ran while one was open for 1% of the time, Pallas kernels for 0%

profile of v2, /device:TPU:0, one launch (start us, length us, event | category | flops | bytes accessed | tf_op | source)
XLA Modules:
  0.0 97.9 jit_solution(18083104482992495631)
XLA Ops:
  6.5 0.0 all-gather.2.cloned.1.call-start
  6.5 1.7 %multiply_reduce_fusion.1 = (f32[112]{0:T(128)S(1)}, f32[112,256]{1,0:T(8,128)}) fusion(f32[112,256]{1,0:T(8,128)} %param.5, f32[256]{0:T(256)} %param.7), kind=kLoop, calls=%fused_computation.29 | loop fusion | flops 85904 | bytes 230848 | tf_op jit(solution)/shard_map/reduce_sum | solution.py:35
  8.2 0.0 all-gather.2.cloned.1.call-update
  8.2 0.5 collective-permute-start
  8.7 1.1 %collective-permute-done = f32[1,112,128]{2,1,0:T(8,128)S(1)} collective-permute-done((f32[1,112,128]{2,1,0:T(8,128)}, f32[1,112,128]{2,1,0:T(8,128)S(1)}, u32[]{:S(2)}, u32[]{:S(2)}) %collective-permute-start) | collective-permute-done | bytes 57376 | tf_op jit(solution)/shard_map/ppermute | solution.py:18
  9.8 0.8 pad_maximum_fusion.4
  10.7 3.0 %collective-permute-start.1 = (f32[2,112,128]{2,1,0:T(8,128)S(1)}, f32[2,112,128]{2,1,0:T(8,128)S(1)}, u32[]{:S(2)}, u32[]{:S(2)}) collective-permute-start(f32[2,112,128]{2,1,0:T(8,128)S(1)} %get-tuple-element.8), channel_id=1, source_target_pairs={{0,2},{1,3},{2,0},{3,1},{4,6},{5,7},{6,4},{7,5},{8,10},{9,11},{10,... | collective-permute-start | bytes 344072 | tf_op jit(solution)/shard_map/ppermute | solution.py:18
  13.7 3.5 %collective-permute-done.1 = f32[2,112,128]{2,1,0:T(8,128)S(1)} collective-permute-done((f32[2,112,128]{2,1,0:T(8,128)S(1)}, f32[2,112,128]{2,1,0:T(8,128)S(1)}, u32[]{:S(2)}, u32[]{:S(2)}) %collective-permute-start.1) | collective-permute-done | bytes 114720 | tf_op jit(solution)/shard_map/ppermute | solution.py:18
  17.2 2.8 %collective-permute-start.2 = (f32[4,112,128]{2,1,0:T(8,128)S(1)}, f32[4,112,128]{2,1,0:T(8,128)S(1)}, u32[]{:S(2)}, u32[]{:S(2)}) collective-permute-start(f32[4,112,128]{2,1,0:T(8,128)S(1)} %bitcast.31), channel_id=1, source_target_pairs={{0,4},{1,5},{2,6},{3,7},{4,0},{5,1},{6,2},{7,3},{8,12},{9,13},{10,... | collective-permute-start | bytes 688136 | tf_op jit(solution)/shard_map/ppermute | solution.py:18
  20.0 12.0 %collective-permute-done.2 = f32[4,112,128]{2,1,0:T(8,128)S(1)} collective-permute-done((f32[4,112,128]{2,1,0:T(8,128)S(1)}, f32[4,112,128]{2,1,0:T(8,128)S(1)}, u32[]{:S(2)}, u32[]{:S(2)}) %collective-permute-start.2) | collective-permute-done | bytes 229408 | tf_op jit(solution)/shard_map/ppermute | solution.py:18
  32.1 1.4 %collective-permute-start.3 = (f32[8,112,128]{2,1,0:T(8,128)S(1)}, f32[8,112,128]{2,1,0:T(8,128)S(1)}, u32[]{:S(2)}, u32[]{:S(2)}) collective-permute-start(f32[8,112,128]{2,1,0:T(8,128)S(1)} %bitcast.28), channel_id=1, source_target_pairs={{0,8},{1,9},{2,10},{3,11},{4,12},{5,13},{6,14},{7,15},{8,0},{9,1},... | collective-permute-start | bytes 1376264 | tf_op jit(solution)/shard_map/ppermute | solution.py:18
  33.4 11.9 %collective-permute-done.3 = f32[8,112,128]{2,1,0:T(8,128)S(1)} collective-permute-done((f32[8,112,128]{2,1,0:T(8,128)S(1)}, f32[8,112,128]{2,1,0:T(8,128)S(1)}, u32[]{:S(2)}, u32[]{:S(2)}) %collective-permute-start.3) | collective-permute-done | bytes 458784 | tf_op jit(solution)/shard_map/ppermute | solution.py:18
  45.3 0.1 pad_maximum_fusion.1
  45.3 0.1 reverse_select_fusion.1
  45.4 1.3 %collective-permute-start.4 = (f32[16,112,128]{2,1,0:T(8,128)S(1)}, f32[16,112,128]{2,1,0:T(8,128)S(1)}, u32[]{:S(2)}, u32[]{:S(2)}) collective-permute-start(f32[16,112,128]{2,1,0:T(8,128)S(1)} %bitcast.26), channel_id=1, source_target_pairs={{0,16},{1,17},{2,18},{3,19},{4,20},{5,21},{6,22},{7,23},{8,24},{9,... | collective-permute-start | bytes 2752520 | tf_op jit(solution)/shard_map/ppermute | solution.py:18
  48.0 18.3 %collective-permute-done.4 = f32[16,112,128]{2,1,0:T(8,128)S(1)} collective-permute-done((f32[16,112,128]{2,1,0:T(8,128)S(1)}, f32[16,112,128]{2,1,0:T(8,128)S(1)}, u32[]{:S(2)}, u32[]{:S(2)}) %collective-permute-start.4) | collective-permute-done | bytes 917536 | tf_op jit(solution)/shard_map/ppermute | solution.py:18
  66.3 0.1 pad_maximum_fusion
  66.4 0.0 copy-start.1
  66.4 0.1 reverse_select_fusion
  66.5 14.6 %all-gather.2.cloned.1.call-done = f32[3584,256]{1,0:T(8,128)} async-done(((f32[112,256]{1,0:T(8,128)}), f32[3584,256]{1,0:T(8,128)}) %all-gather.2.cloned.1.call-update) | async-done | bytes 3670032 | tf_op jit(solution)/shard_map/all_gather | solution.py:56
  81.1 0.0 copy-start
  81.1 2.7 %multiply_reduce_fusion = f32[3584]{0:T(1024)S(1)} fusion(f32[3584,256]{1,0:T(8,128)} %all-gather.2.cloned.1.call-done), kind=kLoop, calls=%fused_computation.5 | loop fusion | flops 1831424 | bytes 3684352 | tf_op jit(solution)/shard_map/reduce_sum | solution.py:35
  83.9 0.0 copy-done.1
  83.9 0.4 copy-done
  84.3 0.0 copy-start.2
  84.3 4.0 %fusion.3 = f32[112,3584]{1,0:T(8,128)S(1)} fusion(f32[112,256]{1,0:T(8,128)S(1)} %copy-done.1, f32[3584,256]{1,0:T(8,128)S(1)} %copy-done, f32[3584]{0:T(1024)S(1)} %multiply_reduce_fusion, f32[112]{0:T(128)S(1)} %get-tuple-element.5), kind=kOutput, calls=%fused_computation.4 | convolution fusion | flops 1235132416 | bytes 5405120 | tf_op jit(solution)/shard_map/dot_general | solution.py:39
  88.3 0.0 copy-done.2
  88.3 2.7 %fusion.13 = f32[112,128]{1,0:T(8,128)} fusion(f32[3584,128]{1,0:T(8,128)S(1)} %bitcast.25, f32[112,3584]{1,0:T(8,128)S(1)} %fusion.3, f32[]{:T(128)} %bitcast.23, f32[112,128]{1,0:T(8,128)S(1)} %copy-done.2, f32[]{:T(128)} %bitcast.24), kind=kOutput, calls=%fused_computation.18 | convolution fusion | flops 619401216 | bytes 3555336 | tf_op jit(solution)/shard_map/dot_general | solution.py:47
  (5 shorter events, 0.1 us)
Async XLA Ops:
  6.5 74.6 %all-gather.2.cloned.1.call-start = ((), (), s32[]{:S(2)}) async-start(), calls=%async_computation | async-start | bytes 3784704 | tf_op jit(solution)/shard_map/all_gather | solution.py:56
  8.2 1.6 %collective-permute-start = (f32[1,112,128]{2,1,0:T(8,128)}, f32[1,112,128]{2,1,0:T(8,128)S(1)}, u32[]{:S(2)}, u32[]{:S(2)}) collective-permute-start(f32[1,112,128]{2,1,0:T(8,128)} %bitcast.35), channel_id=1, source_target_pairs={{0,1},{1,0},{2,3},{3,2},{4,5},{5,4},{6,7},{7,6},{8,9},{9,8},{10,11... | collective-permute-start | bytes 172040 | tf_op jit(solution)/shard_map/ppermute | solution.py:18
  10.7 6.5 %collective-permute-start.1 = (f32[2,112,128]{2,1,0:T(8,128)S(1)}, f32[2,112,128]{2,1,0:T(8,128)S(1)}, u32[]{:S(2)}, u32[]{:S(2)}) collective-permute-start(f32[2,112,128]{2,1,0:T(8,128)S(1)} %get-tuple-element.8), channel_id=1, source_target_pairs={{0,2},{1,3},{2,0},{3,1},{4,6},{5,7},{6,4},{7,5},{8,10},{9,11},{10,... | collective-permute-start | bytes 344072 | tf_op jit(solution)/shard_map/ppermute | solution.py:18
  17.2 14.8 %collective-permute-start.2 = (f32[4,112,128]{2,1,0:T(8,128)S(1)}, f32[4,112,128]{2,1,0:T(8,128)S(1)}, u32[]{:S(2)}, u32[]{:S(2)}) collective-permute-start(f32[4,112,128]{2,1,0:T(8,128)S(1)} %bitcast.31), channel_id=1, source_target_pairs={{0,4},{1,5},{2,6},{3,7},{4,0},{5,1},{6,2},{7,3},{8,12},{9,13},{10,... | collective-permute-start | bytes 688136 | tf_op jit(solution)/shard_map/ppermute | solution.py:18
  32.1 13.2 %collective-permute-start.3 = (f32[8,112,128]{2,1,0:T(8,128)S(1)}, f32[8,112,128]{2,1,0:T(8,128)S(1)}, u32[]{:S(2)}, u32[]{:S(2)}) collective-permute-start(f32[8,112,128]{2,1,0:T(8,128)S(1)} %bitcast.28), channel_id=1, source_target_pairs={{0,8},{1,9},{2,10},{3,11},{4,12},{5,13},{6,14},{7,15},{8,0},{9,1},... | collective-permute-start | bytes 1376264 | tf_op jit(solution)/shard_map/ppermute | solution.py:18
  45.4 20.9 %collective-permute-start.4 = (f32[16,112,128]{2,1,0:T(8,128)S(1)}, f32[16,112,128]{2,1,0:T(8,128)S(1)}, u32[]{:S(2)}, u32[]{:S(2)}) collective-permute-start(f32[16,112,128]{2,1,0:T(8,128)S(1)} %bitcast.26), channel_id=1, source_target_pairs={{0,16},{1,17},{2,18},{3,19},{4,20},{5,21},{6,22},{7,23},{8,24},{9,... | collective-permute-start | bytes 2752520 | tf_op jit(solution)/shard_map/ppermute | solution.py:18
  66.4 17.5 %copy-start.1 = (f32[112,256]{1,0:T(8,128)S(1)}, f32[112,256]{1,0:T(8,128)}, u32[]{:S(2)}) copy-start(f32[112,256]{1,0:T(8,128)} %get-tuple-element.6) | copy-start | bytes 344068
  81.1 3.1 %copy-start = (f32[3584,256]{1,0:T(8,128)S(1)}, f32[3584,256]{1,0:T(8,128)}, u32[]{:S(2)}) copy-start(f32[3584,256]{1,0:T(8,128)} %all-gather.2.cloned.1.call-done) | copy-start | bytes 11010052
  84.3 4.0 %copy-start.2 = (f32[112,128]{1,0:T(8,128)S(1)}, f32[112,128]{1,0:T(8,128)}, u32[]{:S(2)}) copy-start(f32[112,128]{1,0:T(8,128)} %param.6) | copy-start | bytes 172036
Sparse Core Ops, SparseCore 0:
  10.2 70.8 all-gather.1
